TPU v7x, 32 devices: a whole 2x2x4 slice. The times are simulated.
32 devices in a mesh: group: 4 (over y, x), inner: 8 (over z, core).
Axes of the slice: x: 2, y: 2, z: 4, core: 2. Of those that a mesh axis runs over, the one named last changes fastest.
Arguments:
- node_feats: bfloat16 [196608, 256], P(('group', 'inner')), may hold values from -6 to 6
- adj_tiles: bfloat16 [196608, 512], P(('group', 'inner')), may hold values from -0.25 to 0.25
- live_clusters: int32 [32], P(('group', 'inner')), may hold values from 4 to 12, as said below
- req_rows: int32 [32, 32, 16], P(('group', 'inner')), may hold values from 0 to 6143
- req_count: int32 [32, 32], P(('group', 'inner')), may hold values from 0 to 16, as said below
- req_target: int32 [32, 32, 16], P(('group', 'inner')), may hold values from 0 to 6143
- req_weight: float32 [32, 32, 16], P(('group', 'inner')), may hold values from 0.05 to 1
- hist_emb: bfloat16 [196608, 256], P(('group', 'inner')), may hold values from -6 to 6
- hist_grad: bfloat16 [196608, 256], P(('group', 'inner')), may hold values from -6 to 6
- layer_weight: bfloat16 [256, 256], replicated, may hold values from -0.375 to 0.375
- layer_bias: float32 [256], replicated, may hold values from -4 to 4
- cotangent: bfloat16 [196608, 256], P(('group', 'inner')), may hold values from -6 to 6
Outputs:
- input_grad: bfloat16 [196608, 256], P(('group', 'inner'))
- weight_grad: float32 [256, 256], replicated
- bias_grad: float32 [256], replicated
- owner_grad: bfloat16 [196608, 256], P(('group', 'inner'))
Inputs may be any that keep to these rules, and one draw needn't show every extreme that they name: `live_clusters`: some device has all 12 cluster slots filled and some has only the fewest. `req_count`: in every draw each requesting device fills all 16 slots to some owner, and some owner receives 16 used slots from every device.
All inputs are finite; a program needn't handle non-finite values.
Results may differ from a plain program's by a relative error of at most 0.0063.
Values may be sent and summed in bfloat16 or wider, within the bound.
A program may use at most 128 MiB of HBM per device.

v0:
```python
import math

import jax
import jax.numpy as jnp
from jax import lax
from jax.sharding import PartitionSpec as P


def gelu_slope(values):
    root_coef = math.sqrt(2.0 / math.pi)
    cube_coef = 0.044715
    tangent = jnp.tanh(root_coef * (values + cube_coef * values * values * values))
    return 0.5 * (1.0 + tangent) + 0.5 * values * (1.0 - tangent * tangent) * root_coef * (
        1.0 + 3.0 * cube_coef * values * values
    )


def on_device(
    node_feats,
    adj_tiles,
    live_clusters,
    req_rows,
    req_count,
    req_target,
    req_weight,
    hist_emb,
    hist_grad,
    layer_weight,
    layer_bias,
    cotangent,
):
    nodes_dev, width = node_feats.shape
    cluster = adj_tiles.shape[1]
    clusters = nodes_dev // cluster
    asked = req_rows[0]
    peers, slots = asked.shape
    groups = lax.axis_size("group")
    members = lax.axis_size("inner")
    slot_used = jnp.arange(slots)[None, :] < req_count[0][:, None]
    slot_scale = jnp.where(slot_used, req_weight[0], jnp.float32(0.0))
    target_ids = req_target[0]
    targets = target_ids.reshape(-1)
    wanted = lax.all_to_all(asked, ("group", "inner"), split_axis=0, concat_axis=0, tiled=True)
    emb_rows = hist_emb[wanted]
    grad_rows = hist_grad[wanted]
    got_emb = lax.all_to_all(emb_rows, ("group", "inner"), split_axis=0, concat_axis=0, tiled=True)
    got_grad = lax.all_to_all(
        grad_rows, ("group", "inner"), split_axis=0, concat_axis=0, tiled=True
    )
    weights_col = slot_scale.reshape(-1, 1)
    adj_blocks = adj_tiles.reshape(clusters, cluster, cluster)
    local_sum = jnp.einsum(
        "cij,cjf->cif",
        adj_blocks,
        node_feats.reshape(clusters, cluster, width),
        preferred_element_type=jnp.float32,
    ).reshape(nodes_dev, width)
    comp_emb = jax.ops.segment_sum(
        weights_col * got_emb.reshape(-1, width).astype(jnp.float32),
        targets,
        num_segments=nodes_dev,
    )
    aggregate = (local_sum + comp_emb).astype(jnp.bfloat16)
    pre_act = jnp.dot(aggregate, layer_weight, preferred_element_type=jnp.float32) + layer_bias
    live_rows = (jnp.arange(nodes_dev) // cluster < live_clusters[0]).astype(jnp.float32)[:, None]
    grad_pre = cotangent.astype(jnp.float32) * gelu_slope(pre_act) * live_rows
    grad_low = grad_pre.astype(jnp.bfloat16)
    weight_part = jnp.einsum("nf,ng->fg", aggregate, grad_low, preferred_element_type=jnp.float32)
    bias_part = jnp.sum(grad_pre, axis=0)
    feat_grad = jnp.dot(grad_low, layer_weight.T, preferred_element_type=jnp.float32).astype(
        jnp.bfloat16
    )
    message = (slot_scale[:, :, None] * feat_grad[target_ids].astype(jnp.float32)).astype(
        jnp.bfloat16
    )
    arrived = lax.all_to_all(message, ("group", "inner"), split_axis=0, concat_axis=0, tiled=True)
    owner_grad = jax.ops.segment_sum(
        arrived.reshape(-1, width).astype(jnp.float32), wanted.reshape(-1), num_segments=nodes_dev
    ).astype(jnp.bfloat16)
    comp_grad = jax.ops.segment_sum(
        weights_col * got_grad.reshape(-1, width).astype(jnp.float32),
        targets,
        num_segments=nodes_dev,
    ).astype(jnp.bfloat16)
    back_sum = jnp.einsum(
        "cji,cjf->cif",
        adj_blocks,
        feat_grad.reshape(clusters, cluster, width),
        preferred_element_type=jnp.float32,
    ).reshape(nodes_dev, width)
    back_sum = back_sum + jnp.dot(comp_grad, layer_weight.T, preferred_element_type=jnp.float32)
    input_grad = (back_sum * live_rows).astype(jnp.bfloat16)
    weight_sum, bias_sum = lax.psum((weight_part, bias_part), ("group", "inner"))
    norm_factor = float(nodes_dev * groups * members) ** (-0.5)
    return (input_grad, weight_sum * norm_factor, bias_sum * norm_factor, owner_grad)


def solution(mesh):
    return jax.shard_map(
        on_device,
        mesh=mesh,
        in_specs=(
            P(("group", "inner"), None),
            P(("group", "inner"), None),
            P(("group", "inner")),
            P(("group", "inner"), None, None),
            P(("group", "inner"), None),
            P(("group", "inner"), None, None),
            P(("group", "inner"), None, None),
            P(("group", "inner"), None),
            P(("group", "inner"), None),
            P(),
            P(),
            P(("group", "inner"), None),
        ),
        out_specs=(P(("group", "inner"), None), P(), P(), P(("group", "inner"), None)),
        check_vma=False,
    )
```

profile of v0, /device:TPU:0, one launch (start us, length us, event | category | flops | bytes accessed | tf_op | source)
XLA Modules:
  0.0 225.8 jit_solution(15960307121424035594)
XLA Ops:
  7.2 0.0 copy-start
  7.2 1.5 copy.31
  8.7 7.3 %all-to-all-start = ((s32[32,1,16]{2,1,0:T(1,128)}), s32[32,1,16]{2,1,0:T(1,128)S(1)}, u32[]{:S(2)}, u32[]{:S(2)}) async-start(s32[32,1,16]{2,1,0:T(1,128)} %bitcast.4), calls=%async_computation | async-start | bytes 32768 | tf_op jit(solution)/shard_map/all_to_all | solution.py:43
  16.0 0.7 iota_compare_fusion
  16.7 0.7 bitcast_select_fusion
  17.4 0.8 copy.30
  18.8 0.1 copy.29
  18.9 0.1 lt.61
  19.0 0.8 copy.28
  19.8 0.1 reshape.183
  19.9 0.1 squeeze.12
  19.9 0.6 fusion.28
  20.6 0.1 reshape.191
  20.6 0.7 copy.34
  21.3 1.8 all-to-all-done
  23.1 0.1 reshape.167
  23.2 4.5 %gather_fusion = bf16[512,256]{1,0:T(8,128)(2,1)} fusion(bf16[6144,256]{1,0:T(8,128)(2,1)} %param.19, s32[1024]{0:T(1024)S(1)} %pad_clamp_fusion.1), kind=kCustom, calls=%fused_computation | custom fusion | bytes 526336 | tf_op jit(solution)/shard_map/gather | solution.py:44
  27.7 4.1 %all-to-all-start.1 = ((bf16[32,16,256]{2,1,0:T(8,128)(2,1)}), bf16[32,16,256]{2,1,0:T(8,128)(2,1)S(1)}, u32[]{:S(2)}, u32[]{:S(2)}) async-start(bf16[32,16,256]{2,1,0:T(8,128)(2,1)} %bitcast.48), calls=%async_computation.1 | async-start | bytes 524288 | tf_op jit(solution)/shard_map/all_to_all | solution.py:46
  31.8 7.2 %fusion.30 = f32[12,512,256]{2,1,0:T(8,128)} fusion(bf16[12,512,512]{2,1,0:T(8,128)(2,1)} %bitcast.40, bf16[12,512,256]{2,1,0:T(8,128)(2,1)S(1)} %bitcast.39), kind=kOutput, calls=%fused_computation.58 | convolution fusion | flops 1610612736 | bytes 15728640 | tf_op jit(solution)/shard_map/cij,cjf->cif/dot_general | solution.py:52
  39.0 0.5 broadcast.135
  39.5 2.0 reduce.3
  41.5 1.4 reshape.207
  42.9 4.5 %gather_fusion.1 = bf16[512,256]{1,0:T(8,128)(2,1)} fusion(bf16[6144,256]{1,0:T(8,128)(2,1)} %param.20, s32[1024]{0:T(1024)S(1)} %pad_clamp_fusion.1), kind=kCustom, calls=%fused_computation.1 | custom fusion | bytes 526336 | tf_op jit(solution)/shard_map/gather | solution.py:45
  47.4 0.0 all-to-all-done.1
  47.4 0.7 copy-done.3
  48.1 5.8 %all-to-all-start.2 = ((bf16[32,16,256]{2,1,0:T(8,128)(2,1)}), bf16[32,16,256]{2,1,0:T(8,128)(2,1)S(1)}, u32[]{:S(2)}, u32[]{:S(2)}) async-start(bf16[32,16,256]{2,1,0:T(8,128)(2,1)} %bitcast.46), calls=%async_computation.2 | async-start | bytes 524288 | tf_op jit(solution)/shard_map/all_to_all | solution.py:47
  54.0 0.0 all-reduce.2.cloned.1.call-start
  54.0 9.0 %scatter_custom_fusion = f32[6144,256]{1,0:T(8,128)} fusion(f32[6144,256]{1,0:T(8,128)} %bitcast.42, s32[512]{0:T(512)S(1)} %reshape.191, bf16[512,256]{1,0:T(8,128)(2,1)} %bitcast.47, f32[512]{0:T(512)S(1)} %broadcast_select_fusion), kind=kCustom, calls=%fused_computation.36 | custom fusion | flops 393216 | bytes 6555648 | tf_op jit(solution)/shard_map/scatter-add | solution.py:58
  63.0 8.5 %fusion.29 = (f32[256]{0:T(256)}, bf16[6144,256]{1,0:T(8,128)(2,1)S(1)}) fusion(f32[6144]{0:T(1024)} %fusion.28, f32[256]{0:T(256)} %param.22, bf16[256,256]{1,0:T(8,128)(2,1)S(1)} %copy-done.4, f32[6144,256]{1,0:T(8,128)} %scatter_custom_fusion, bf16[6144,256]{1,0:T(8,128)(2,1)} %param.23), kind=kOutput, calls=%fused_computation.57 | convolution fusion | flops 843054848 | bytes 12740608 | tf_op jit(solution)/shard_map/dot_general | solution.py:64
  71.4 1.7 copy-done.2
  73.1 1.7 fusion.14
  74.8 4.6 %convolution_convert_fusion = bf16[6144,256]{1,0:T(8,128)(2,1)} fusion(bf16[256,256]{1,0:T(8,128)(2,1)S(1)} %copy-done.4, bf16[6144,256]{1,0:T(8,128)(2,1)} %copy-done.2), kind=kOutput, calls=%fused_computation.12 | convolution fusion | flops 806879232 | bytes 6422528 | tf_op jit(solution)/shard_map/dot_general | solution.py:70
  79.4 0.0 all-reduce.2.cloned.1.call-update
  79.4 8.2 %convolution_bitcast_fusion = f32[12,512,256]{1,2,0:T(8,128)} fusion(bf16[12,512,256]{2,1,0:T(8,128)(2,1)} %bitcast.43, bf16[12,512,512]{2,1,0:T(8,128)(2,1)} %bitcast.41), kind=kOutput, calls=%fused_computation.25 | convolution fusion | flops 1610612736 | bytes 15728640 | tf_op jit(solution)/shard_map/cji,cjf->cif/dot_general | solution.py:85
  87.7 4.5 %gather_fusion.2 = bf16[512,256]{1,0:T(8,128)(2,1)} fusion(bf16[6144,256]{1,0:T(8,128)(2,1)} %convolution_convert_fusion, s32[1024]{0:T(1024)S(1)} %pad_clamp_fusion), kind=kCustom, calls=%fused_computation.2 | custom fusion | bytes 526336 | tf_op jit(solution)/shard_map/gather | solution.py:73
  92.2 6.6 %copy.33 = f32[12,512,256]{2,1,0:T(8,128)} copy(f32[12,512,256]{1,2,0:T(8,128)} %convolution_bitcast_fusion) | data formatting | bytes 12582912 | tf_op jit(solution)/shard_map/cji,cjf->cif/dot_general | solution.py:85
  98.8 1.8 fusion.20
  100.5 0.0 all-to-all-done.2
  100.5 6.0 %all-to-all-start.3 = ((bf16[32,16,256]{2,1,0:T(8,128)(2,1)}), bf16[32,16,256]{2,1,0:T(8,128)(2,1)}, u32[]{:S(2)}, u32[]{:S(2)}) async-start(bf16[32,16,256]{2,1,0:T(8,128)(2,1)} %fusion.20), calls=%async_computation.3 | async-start | bytes 524288 | tf_op jit(solution)/shard_map/all_to_all | solution.py:76
  106.5 6.6 %scatter_custom_fusion.1 = f32[6144,256]{1,0:T(8,128)} fusion(s32[512]{0:T(512)} %copy-done.8, f32[]{:T(128)} %constant.13.clone.1, bf16[512,256]{1,0:T(8,128)(2,1)S(1)} %bitcast.45, f32[512]{0:T(512)} %copy-done.7), kind=kCustom, calls=%fused_computation.23 | custom fusion | flops 393216 | bytes 6556160 | tf_op jit(solution)/shard_map/scatter-add | solution.py:80
  113.1 7.6 %fusion.1 = bf16[6144,256]{1,0:T(8,128)(2,1)} fusion(f32[6144,256]{1,0:T(8,128)} %bitcast.44, bf16[256,256]{1,0:T(8,128)(2,1)S(1)} %copy-done.4, f32[6144,256]{1,0:T(8,128)} %scatter_custom_fusion.1, f32[6144]{0:T(1024)} %fusion.28), kind=kOutput, calls=%fused_computation.11 | convolution fusion | flops 811597824 | bytes 15884288 | tf_op jit(solution)/shard_map/dot_general | solution.py:91
  120.7 40.5 %psum.15 = f32[256]{0:T(256)S(1)} all-reduce(f32[256]{0:T(256)S(1)} %copy-done.9), channel_id=1, replica_groups=mesh['group'=4,'inner'=8] {'group','inner'}, use_global_device_ids=true, to_apply=%region_4.5 | all-reduce | flops 256 | bytes 2048 | tf_op jit(solution)/shard_map/psum | solution.py:93
  161.2 0.6 broadcast_multiply_fusion.1
  161.7 44.1 %all-reduce.2.cloned.1.call-done = f32[256,256]{1,0:T(8,128)} async-done(((f32[256,256]{1,0:T(8,128)}), f32[256,256]{1,0:T(8,128)}) %all-reduce.2.cloned.1.call-update) | async-done | bytes 262160 | tf_op jit(solution)/shard_map/psum | solution.py:93
  205.8 1.7 broadcast_multiply_fusion
  207.5 0.0 all-to-all-done.3
  207.5 6.7 %scatter_custom_fusion.2 = f32[6144,256]{1,0:T(8,128)} fusion(s32[512]{0:T(512)} %reshape.207, f32[]{:T(128)} %constant.13.clone.1, bf16[512,256]{1,0:T(8,128)(2,1)} %bitcast.21), kind=kCustom, calls=%fused_computation.21 | custom fusion | flops 262144 | bytes 6554112 | tf_op jit(solution)/shard_map/scatter-add | solution.py:77
  214.2 4.8 %convert_element_type.67 = bf16[6144,256]{1,0:T(8,128)(2,1)} convert(f32[6144,256]{1,0:T(8,128)} %scatter_custom_fusion.2) | non-fusion elementwise | flops 1572864 | bytes 9437184 | tf_op jit(solution)/shard_map/convert_element_type | solution.py:79
  (22 shorter events, 0.1 us)
Async XLA Ops:
  7.2 24.6 %copy-start = (bf16[6144,256]{1,0:T(8,128)(2,1)S(1)}, bf16[6144,256]{1,0:T(8,128)(2,1)}, u32[]{:S(2)}) copy-start(bf16[6144,256]{1,0:T(8,128)(2,1)} %param.12) | copy-start | bytes 9437188
  8.7 14.4 %all-to-all-start = ((s32[32,1,16]{2,1,0:T(1,128)}), s32[32,1,16]{2,1,0:T(1,128)S(1)}, u32[]{:S(2)}, u32[]{:S(2)}) async-start(s32[32,1,16]{2,1,0:T(1,128)} %bitcast.4), calls=%async_computation | async-start | bytes 32768 | tf_op jit(solution)/shard_map/all_to_all | solution.py:43
  20.5 33.5 %copy-start.7 = (f32[512]{0:T(512)}, f32[512]{0:T(512)S(1)}, u32[]{:S(2)}) copy-start(f32[512]{0:T(512)S(1)} %broadcast_select_fusion) | copy-start | bytes 6148
  20.6 33.4 %copy-start.8 = (s32[512]{0:T(512)}, s32[512]{0:T(512)S(1)}, u32[]{:S(2)}) copy-start(s32[512]{0:T(512)S(1)} %reshape.191) | copy-start | bytes 6148
  23.1 4.6 %copy-start.5 = (s32[32,1,16]{2,1,0:T(1,128)}, s32[32,1,16]{2,1,0:T(1,128)S(1)}, u32[]{:S(2)}) copy-start(s32[32,1,16]{2,1,0:T(1,128)S(1)} %all-to-all-done) | copy-start | bytes 6148
  27.7 19.7 %all-to-all-start.1 = ((bf16[32,16,256]{2,1,0:T(8,128)(2,1)}), bf16[32,16,256]{2,1,0:T(8,128)(2,1)S(1)}, u32[]{:S(2)}, u32[]{:S(2)}) async-start(bf16[32,16,256]{2,1,0:T(8,128)(2,1)} %bitcast.48), calls=%async_computation.1 | async-start | bytes 524288 | tf_op jit(solution)/shard_map/all_to_all | solution.py:46
  39.0 24.0 %copy-start.4 = (bf16[256,256]{1,0:T(8,128)(2,1)S(1)}, bf16[256,256]{1,0:T(8,128)(2,1)}, u32[]{:S(2)}) copy-start(bf16[256,256]{1,0:T(8,128)(2,1)} %param.21) | copy-start | bytes 393220
  47.4 0.7 copy-start.3
  48.1 52.4 %all-to-all-start.2 = ((bf16[32,16,256]{2,1,0:T(8,128)(2,1)}), bf16[32,16,256]{2,1,0:T(8,128)(2,1)S(1)}, u32[]{:S(2)}, u32[]{:S(2)}) async-start(bf16[32,16,256]{2,1,0:T(8,128)(2,1)} %bitcast.46), calls=%async_computation.2 | async-start | bytes 524288 | tf_op jit(solution)/shard_map/all_to_all | solution.py:47
  54.0 151.8 %all-reduce.2.cloned.1.call-start = ((), (), s32[]{:S(2)}) async-start(), calls=%async_computation.4 | async-start | bytes 524288 | tf_op jit(solution)/shard_map/psum | solution.py:93
  63.0 10.1 %copy-start.1 = (f32[6144,256]{1,0:T(8,128)S(1)}, f32[6144,256]{1,0:T(8,128)}, u32[]{:S(2)}) copy-start(f32[6144,256]{1,0:T(8,128)} %scatter_custom_fusion) | copy-start | bytes 18874372
  71.4 1.7 copy-start.2
  92.1 6.6 %copy-start.6 = (f32[32,16]{1,0:T(8,128)S(1)}, f32[32,16]{1,0:T(8,128)}, u32[]{:S(2)}) copy-start(f32[32,16]{1,0:T(8,128)} %copy.34) | copy-start | bytes 6148
  100.5 106.9 %all-to-all-start.3 = ((bf16[32,16,256]{2,1,0:T(8,128)(2,1)}), bf16[32,16,256]{2,1,0:T(8,128)(2,1)}, u32[]{:S(2)}, u32[]{:S(2)}) async-start(bf16[32,16,256]{2,1,0:T(8,128)(2,1)} %fusion.20), calls=%async_computation.3 | async-start | bytes 524288 | tf_op jit(solution)/shard_map/all_to_all | solution.py:76
  113.1 7.6 %copy-start.9 = (f32[256]{0:T(256)S(1)}, f32[256]{0:T(256)}, u32[]{:S(2)}) copy-start(f32[256]{0:T(256)} %get-tuple-element.4) | copy-start | bytes 3076
Sparse Core Ops, SparseCore 0:
  79.5 126.2 all-reduce.1
where the time goes:
time: 227 us; the launch traced here: 226 us
  waiting for transfers between devices  45.8 us (20%)
  blocking collectives  40.5 us (18%)
  matrix products  37.8 us (17%)
  other arithmetic  35.1 us (15%)
  local copies, waits for them, and re-layouts  28.6 us (13%)
  starting transfers between devices  23.2 us (10%)
  between operations  14.8 us (7%)
    psum x1, waiting for transfers between devices, on_device(): lax.psum((weight_part, bias_part), ('group', 'inner'))  44.1 us
    psum x1, blocking collectives, on_device(): lax.psum((weight_part, bias_part), ('group', 'inner'))  40.5 us
    scatter-add x1, other arithmetic, on_device(): jax.ops.segment_sum(weights_col * got_emb.reshape(-1, width).astype(jnp.f...  8.96 us
    dot_general x1, matrix products, on_device(): jnp.dot(aggregate, layer_weight, preferred_element_type=jnp.float32)  8.45 us
    dot_general x1, matrix products, on_device(): jnp.einsum('cji,cjf->cif', adj_blocks, feat_grad.reshape(clusters, cluste...  8.25 us
    dot_general x1, matrix products, on_device(): jnp.dot(comp_grad, layer_weight.T, preferred_element_type=jnp.float32)  7.58 us
    all_to_all x1, starting transfers between devices, on_device(): lax.all_to_all(asked, ('group', 'inner'), split_axis=0, concat_axis=0, ti...  7.3 us
    dot_general x1, matrix products, on_device(): jnp.einsum('cij,cjf->cif', adj_blocks, node_feats.reshape(clusters, clust...  7.24 us
  transfers between devices with their start and end apart: 5, of which 2 were waited for; matrix products, arithmetic and copies ran while one was open for 36% of the time, Pallas kernels for 0%

commit v1 on v0

v1 whole, which is shorter than its diff:
```python
import functools
import math

import jax
import jax.numpy as jnp
from jax import lax
from jax.experimental import pallas as pl
from jax.experimental.pallas import tpu as pltpu
from jax.sharding import PartitionSpec as P

MESH = pl.DeviceIdType.MESH
BF = jnp.bfloat16
F32 = jnp.float32
NN = (((1,), (0,)), ((), ()))
NT = (((1,), (1,)), ((), ()))
TN = (((0,), (0,)), ((), ()))


def mm(a, b, dims=NN):
    return lax.dot_general(a, b, dims, preferred_element_type=F32)


def exact(a, b, dims=NN):
    return lax.dot_general(
        a, b, dims, preferred_element_type=F32, precision=lax.Precision.HIGHEST
    )


def iota(shape, dim):
    return lax.broadcasted_iota(jnp.int32, shape, dim)


def gelu_slope(z):
    root = math.sqrt(2.0 / math.pi)
    cube = 0.044715
    sq = z * z
    t = jnp.tanh(root * z * (1.0 + cube * sq))
    return 0.5 * (1.0 + t) + (0.5 * root) * z * (1.0 - t * t) * (1.0 + 3.0 * cube * sq)


def column_of(table, slots):
    peers = table.shape[1]
    total = peers * slots
    pick = (iota((total, slots), 0) % slots == iota((total, slots), 1)).astype(F32)
    wide = exact(pick, table)
    keep = iota((total, peers), 0) // slots == iota((total, peers), 1)
    return jnp.sum(jnp.where(keep, wide, 0.0), axis=1, keepdims=True)


def row_of(table, slots):
    peers = table.shape[1]
    total = peers * slots
    pick = (iota((peers, total), 1) // slots == iota((peers, total), 0)).astype(F32)
    wide = exact(table, pick)
    keep = iota((slots, total), 1) % slots == iota((slots, total), 0)
    return jnp.sum(jnp.where(keep, wide, 0.0), axis=0, keepdims=True)


def main_kernel(
    members, peers, reducers,
    live_ref, rows_ref, count_ref, target_ref, weight_ref, w_ref, bias_ref,
    feats_hbm, adj_hbm, cot_hbm, emb_hbm, grad_hbm,
    wanted_out, arrived_out, wg_out, bg_out, ig_hbm,
    feats, adj, cot, emb, grad, local, fg, ig,
    rq_send, rq_recv, e_send, e_recv, g_send, g_recv, m_send,
    rs_send, rs_recv, acc, mes, wacc, bacc,
    load_sem, adj_sem, out_sem, send_sem, recv_sem,
):
    nodes_dev, width = feats.shape
    cluster = adj.shape[1]
    clusters = nodes_dev // cluster
    slots = rows_ref.shape[0]
    total = peers * slots
    me = lax.axis_index("group") * members + lax.axis_index("inner")
    part = width // reducers
    chunk = rs_send.shape[0] // reducers

    def at(p):
        return (p // members, p % members)

    def tile(ref, c):
        return ref.at[pl.ds(pl.multiple_of(c * cluster, cluster), cluster)]

    loads = [
        pltpu.make_async_copy(src, dst, load_sem.at[i])
        for i, (src, dst) in enumerate(
            ((feats_hbm, feats), (emb_hbm, emb), (grad_hbm, grad), (cot_hbm, cot))
        )
    ]

    def adj_load(c):
        return pltpu.make_async_copy(tile(adj_hbm, c), tile(adj, c), adj_sem.at[c])

    loads[0].start()
    for c in range(clusters):
        adj_load(c).start()
    loads[1].start()
    loads[2].start()
    loads[3].start()

    barrier = pltpu.get_barrier_semaphore()

    @pl.loop(1, peers)
    def _(i):
        pl.semaphore_signal(
            barrier, inc=1, device_id=at(lax.rem(me + i, peers)), device_id_type=MESH
        )

    rows = rows_ref[...].astype(F32)
    rows = jnp.concatenate([rows, jnp.zeros((128 - slots, peers), F32)], axis=0)
    eye = (iota((peers, peers), 0) == iota((peers, peers), 1)).astype(F32)
    by_owner = exact(eye, rows, NT)
    for p in range(peers):
        rq_send[p] = by_owner[p : p + 1, :]
    rq_recv[me] = rq_send[me]

    pl.semaphore_wait(barrier, peers - 1)

    def to_all(phase, src_of, dst_of):
        @pl.loop(1, peers)
        def _(i):
            p = lax.rem(me + i, peers)
            pltpu.make_async_remote_copy(
                src_ref=src_of(p),
                dst_ref=dst_of(me),
                send_sem=send_sem.at[phase],
                recv_sem=recv_sem.at[phase],
                device_id=at(p),
                device_id_type=MESH,
            ).start()

    def wait_bytes(ref, sem):
        pltpu.make_async_copy(ref, ref, sem).wait()

    def rows_at(ref, size):
        return lambda p: ref.at[pl.ds(pl.multiple_of(p * size, size), size)]

    to_all(0, lambda p: rq_send.at[p], lambda p: rq_recv.at[p])

    loads[0].wait()

    @pl.loop(0, clusters)
    def _(c):
        adj_load(c).wait()
        tile(local, c)[...] = mm(tile(adj, c)[...], tile(feats, c)[...])

    wait_bytes(rq_recv.at[pl.ds(0, peers - 1)], recv_sem.at[0])
    wanted = jnp.concatenate([rq_recv[p] for p in range(peers)], axis=0)
    wanted_out[...] = wanted
    pick = (iota((total, peers), 0) // slots == iota((total, peers), 1)).astype(F32)
    wide = exact(pick, wanted)
    keep = iota((total, 128), 0) % slots == iota((total, 128), 1)
    wanted_col = jnp.sum(jnp.where(keep, wide, 0.0), axis=1, keepdims=True).astype(jnp.int32)
    lane = iota((total, cluster), 1)

    def gather(table, out):
        acc[...] = jnp.zeros_like(acc)

        @pl.loop(0, clusters)
        def _(c):
            one = jnp.where(wanted_col - c * cluster == lane, 1.0, 0.0).astype(BF)
            acc[...] += mm(one, tile(table, c)[...])

        out[...] = acc[...].astype(BF)

    own = pl.ds(pl.multiple_of(me * slots, slots), slots)
    loads[1].wait()
    gather(emb, e_send)
    e_recv[own, :] = e_send[own, :]
    to_all(1, rows_at(e_send, slots), rows_at(e_recv, slots))
    loads[2].wait()
    gather(grad, g_send)
    g_recv[own, :] = g_send[own, :]
    to_all(2, rows_at(g_send, slots), rows_at(g_recv, slots))

    used = iota((slots, peers), 0) < count_ref[...]
    scale_col = column_of(jnp.where(used, weight_ref[...], 0.0), slots)
    targets = target_ref[...].astype(F32)
    target_col = column_of(targets, slots).astype(jnp.int32)
    target_row = row_of(targets, slots).astype(jnp.int32)
    node = iota((cluster, total), 0)
    weights = w_ref[...]
    bias = bias_ref[...]
    mes[...] = jnp.zeros_like(mes)
    wacc[...] = jnp.zeros_like(wacc)
    bacc[...] = jnp.zeros_like(bacc)
    loads[3].wait()

    wait_bytes(e_recv.at[pl.ds(0, (peers - 1) * slots)], recv_sem.at[1])
    e_recv[...] = (scale_col * e_recv[...].astype(F32)).astype(BF)

    def live_of(c):
        return jnp.where(c < live_ref[0], 1.0, 0.0).astype(F32)

    @pl.loop(0, clusters)
    def _(c):
        spread = jnp.where(target_row - c * cluster == node, 1.0, 0.0).astype(BF)
        agg = (tile(local, c)[...] + mm(spread, e_recv[...])).astype(BF)
        pre = mm(agg, weights) + bias
        g = tile(cot, c)[...].astype(F32) * gelu_slope(pre) * live_of(c)
        low = g.astype(BF)
        bacc[...] += jnp.sum(g.reshape(cluster // 8, 8, width), axis=0)
        wacc[...] += mm(agg, low, TN)
        back = mm(low, weights, NT).astype(BF)
        tile(fg, c)[...] = back
        take = jnp.where(target_col - c * cluster == lane, 1.0, 0.0).astype(BF)
        mes[...] += mm(take, back)

    sums = bacc[...].astype(BF).astype(F32)
    for r in range(reducers):
        piece = wacc[r * part : (r + 1) * part, :]
        fill = chunk - part - 8
        both = [piece, sums] + ([jnp.zeros((fill, width), F32)] if fill else [])
        rs_send[r * chunk : (r + 1) * chunk, :] = jnp.concatenate(both, axis=0).astype(BF)
    slice_of = rows_at(rs_send, chunk)
    slot_of = rows_at(rs_recv, chunk)
    slot_of(me)[...] = slice_of(lax.rem(me, reducers))[...]
    to_all(3, lambda p: slice_of(lax.rem(p, reducers)), slot_of)
    m_send[...] = (scale_col * mes[...]).astype(BF)
    arrived_out[own, :] = m_send[own, :]
    to_all(4, rows_at(m_send, slots), rows_at(arrived_out, slots))

    wait_bytes(g_recv.at[pl.ds(0, (peers - 1) * slots)], recv_sem.at[2])
    scaled = (scale_col * g_recv[...].astype(F32)).astype(BF)
    e_recv[...] = mm(scaled, weights, NT).astype(BF)

    def out_copy(c):
        return pltpu.make_async_copy(tile(ig, c), tile(ig_hbm, c), out_sem)

    def backward(c):
        spread = jnp.where(target_row - c * cluster == node, 1.0, 0.0).astype(BF)
        back = mm(tile(adj, c)[...], tile(fg, c)[...], TN) + mm(spread, e_recv[...])
        tile(ig, c)[...] = (back * live_of(c)).astype(BF)
        out_copy(c).start()

    half = clusters // 2

    @pl.loop(0, half)
    def _(c):
        backward(c)

    wait_bytes(rs_recv.at[pl.ds(0, (peers - 1) * chunk)], recv_sem.at[3])
    norm = float(nodes_dev * peers) ** (-0.5)
    got = jnp.sum(rs_recv[...].astype(F32).reshape(peers, chunk, width), axis=0) * norm
    mine = lax.rem(me, reducers)
    part_of = rows_at(wg_out, part)
    part_of(mine)[...] = got[:part, :]
    bg_out[...] = jnp.sum(got[part : part + 8, :], axis=0, keepdims=True)

    def share():
        to_all(5, lambda p: part_of(me), part_of)

    if reducers == peers:
        share()
    else:
        pl.when(me < reducers)(share)

    @pl.loop(half, clusters)
    def _(c):
        backward(c)

    if reducers == peers:
        wait_bytes(wg_out.at[pl.ds(0, (peers - 1) * part)], recv_sem.at[5])
        wait_bytes(wg_out.at[pl.ds(0, (peers - 1) * part)], send_sem.at[5])
    else:
        @pl.when(me < reducers)
        def _():
            wait_bytes(wg_out.at[pl.ds(0, (reducers - 1) * part)], recv_sem.at[5])

            @pl.loop(1, peers)
            def _(i):
                wait_bytes(wg_out.at[pl.ds(0, part)], send_sem.at[5])

        @pl.when(me >= reducers)
        def _():
            wait_bytes(wg_out, recv_sem.at[5])

    wait_bytes(arrived_out.at[pl.ds(0, (peers - 1) * slots)], recv_sem.at[4])
    wait_bytes(rq_send.at[pl.ds(0, peers - 1)], send_sem.at[0])
    wait_bytes(e_send.at[pl.ds(0, (peers - 1) * slots)], send_sem.at[1])
    wait_bytes(g_send.at[pl.ds(0, (peers - 1) * slots)], send_sem.at[2])
    wait_bytes(rs_recv.at[pl.ds(0, (peers - 1) * chunk)], send_sem.at[3])
    wait_bytes(m_send.at[pl.ds(0, (peers - 1) * slots)], send_sem.at[4])
    wait_bytes(ig, out_sem)


def owner_kernel(slots, wanted_ref, arrived_ref, ig_ref, out_ref, ig_out, row_scr):
    step = pl.program_id(0)
    peers = wanted_ref.shape[0]
    total = peers * slots

    @pl.when(step == 0)
    def _():
        pick = (iota((peers, total), 1) // slots == iota((peers, total), 0)).astype(F32)
        wide = exact(wanted_ref[...], pick, TN)
        keep = iota((128, total), 1) % slots == iota((128, total), 0)
        row = jnp.sum(jnp.where(keep, wide, 0.0), axis=0, keepdims=True)
        row_scr[...] = row.astype(jnp.int32)

    size = out_ref.shape[0]
    spread = jnp.where(row_scr[...] - step * size == iota((size, total), 0), 1.0, 0.0)
    out_ref[...] = mm(spread.astype(BF), arrived_ref[...]).astype(BF)
    ig_out[...] = ig_ref[...]


def on_device(
    node_feats, adj_tiles, live_clusters, req_rows, req_count, req_target, req_weight,
    hist_emb, hist_grad, layer_weight, layer_bias, cotangent,
):
    nodes_dev, width = node_feats.shape
    cluster = adj_tiles.shape[1]
    clusters = nodes_dev // cluster
    peers, slots = req_rows.shape[1:]
    members = lax.axis_size("inner")
    total = peers * slots
    reducers = min(peers, 32)
    part = width // reducers
    chunk = -(-(part + 8) // 16) * 16
    flip = lambda a: jnp.transpose(a[0])
    vmem = pl.BlockSpec(memory_space=pltpu.VMEM)
    hbm = pl.BlockSpec(memory_space=pl.ANY)
    sds = jax.ShapeDtypeStruct
    full = (nodes_dev, width)
    wanted, arrived, wg, bg, ig = pl.pallas_call(
        functools.partial(main_kernel, members, peers, reducers),
        out_shape=(
            sds((peers, 128), F32),
            sds((total, width), BF),
            sds((width, width), F32),
            sds((1, width), F32),
            sds(full, BF),
        ),
        in_specs=[pl.BlockSpec(memory_space=pltpu.SMEM)] + [vmem] * 6 + [hbm] * 5,
        out_specs=(vmem, vmem, vmem, vmem, hbm),
        scratch_shapes=[
            pltpu.VMEM(full, BF),
            pltpu.VMEM((nodes_dev, cluster), BF),
            pltpu.VMEM(full, BF),
            pltpu.VMEM(full, BF),
            pltpu.VMEM(full, BF),
            pltpu.VMEM(full, F32),
            pltpu.VMEM(full, BF),
            pltpu.VMEM(full, BF),
            pltpu.VMEM((peers, 1, 128), F32),
            pltpu.VMEM((peers, 1, 128), F32),
            pltpu.VMEM((total, width), BF),
            pltpu.VMEM((total, width), BF),
            pltpu.VMEM((total, width), BF),
            pltpu.VMEM((total, width), BF),
            pltpu.VMEM((total, width), BF),
            pltpu.VMEM((reducers * chunk, width), BF),
            pltpu.VMEM((peers * chunk, width), BF),
            pltpu.VMEM((total, width), F32),
            pltpu.VMEM((total, width), F32),
            pltpu.VMEM((width, width), F32),
            pltpu.VMEM((8, width), F32),
            pltpu.SemaphoreType.DMA((4,)),
            pltpu.SemaphoreType.DMA((clusters,)),
            pltpu.SemaphoreType.DMA,
            pltpu.SemaphoreType.DMA((6,)),
            pltpu.SemaphoreType.DMA((6,)),
        ],
        compiler_params=pltpu.CompilerParams(
            collective_id=0, has_side_effects=True, vmem_limit_bytes=58 * 1024 * 1024
        ),
    )(
        live_clusters, flip(req_rows), req_count, flip(req_target), flip(req_weight),
        layer_weight, layer_bias[None, :],
        node_feats, adj_tiles, cotangent, hist_emb, hist_grad,
    )
    whole = lambda a: pl.BlockSpec(a.shape, lambda i: (0, 0))
    tiles = pl.BlockSpec((cluster, width), lambda i: (i, 0))
    owner_grad, input_grad = pl.pallas_call(
        functools.partial(owner_kernel, slots),
        grid=(clusters,),
        out_shape=(sds(full, BF), sds(full, BF)),
        in_specs=[whole(wanted), whole(arrived), tiles],
        out_specs=(tiles, tiles),
        scratch_shapes=[pltpu.VMEM((1, total), jnp.int32)],
        compiler_params=pltpu.CompilerParams(vmem_limit_bytes=32 * 1024 * 1024),
    )(wanted, arrived, ig)
    return input_grad, wg, bg[0], owner_grad


def solution(mesh):
    both = ("group", "inner")
    return jax.shard_map(
        on_device,
        mesh=mesh,
        in_specs=(
            P(both, None), P(both, None), P(both), P(both, None, None), P(both, None),
            P(both, None, None), P(both, None, None), P(both, None), P(both, None),
            P(), P(), P(both, None),
        ),
        out_specs=(P(both, None), P(), P(), P(both, None)),
        check_vma=False,
    )
```

time: 227 us -> 74.1 us (0.33)
  Pallas kernels: 0 us -> 67.7 us
  waiting for transfers between devices: 45.8 us -> 0 us
  blocking collectives: 40.5 us -> 0 us
  matrix products: 37.8 us -> 0 us
  other arithmetic: 35.1 us -> 0 us
  local copies, waits for them, and re-layouts: 28.6 us -> 4.82 us
  starting transfers between devices: 23.2 us -> 0 us
  between operations: 14.8 us -> 1.31 us
    pallas_call x0 -> x2, Pallas kernels: none -> 67.7 us  [the longest x1 60.9 us: on_device(): pl.pallas_call(functools.partial(main_kernel, members, peers, reducers),...]
    psum x1 -> x0, waiting for transfers between devices: 44.1 us -> none  [on_device(): lax.psum((weight_part, bias_part), ('group', 'inner'))]
    psum x1 -> x0, blocking collectives: 40.5 us -> none  [on_device(): lax.psum((weight_part, bias_part), ('group', 'inner'))]
    dot_general x6 -> x0, matrix products: 37.8 us -> none  [the longest x1 8.45 us: on_device(): jnp.dot(aggregate, layer_weight, preferred_element_type=jnp.float32)]
    all_to_all x4 -> x0, starting transfers between devices: 23.2 us -> none  [the longest x1 7.3 us: on_device(): lax.all_to_all(asked, ('group', 'inner'), split_axis=0, concat_axis=0, ti...]
    scatter-add x3 -> x0, other arithmetic: 22.3 us -> none  [the longest x1 8.96 us: on_device(): jax.ops.segment_sum(weights_col * got_emb.reshape(-1, width).astype(jnp.f...]
    gather x3 -> x0, local copies, waits for them, and re-layouts: 13.5 us -> none  [the longest x1 4.49 us: on_device(): emb_rows = hist_emb[wanted]]
    convert_element_type x3 -> x0, other arithmetic: 7.15 us -> none  [the longest x1 4.75 us: on_device(): owner_grad = jax.ops.segment_sum(arrived.reshape(-1, width).astype(jnp.fl...]
  transfers between devices with their start and end apart: 5 -> 0, of which waited for: 2 -> 0; matrix products, arithmetic and copies ran while one was open for 36% -> 0% of each run, Pallas kernels for 0% -> 0%
where the time goes in v1:
time: 74.1 us; the launch traced here: 73.9 us
  Pallas kernels  67.7 us (91%)
  local copies, waits for them, and re-layouts  4.82 us (7%)
  between operations  1.31 us (2%)
    pallas_call x1, Pallas kernels, on_device(): pl.pallas_call(functools.partial(main_kernel, members, peers, reducers),...  60.9 us
    pallas_call x1, Pallas kernels, on_device(): pl.pallas_call(functools.partial(owner_kernel, slots), grid=(clusters,),...  6.85 us
    unnamed x12, local copies, waits for them, and re-layouts  4.82 us

profile of v1, /device:TPU:0, one launch (start us, length us, event | category | flops | bytes accessed | tf_op | source)
XLA Modules:
  0.0 73.9 jit_solution(13992831829766796789)
XLA Ops:
  1.3 60.9 %shard_map.147 = (f32[32,128]{1,0:T(8,128)}, bf16[512,256]{1,0:T(8,128)(2,1)}, f32[256,256]{1,0:T(8,128)}, f32[1,256]{1,0:T(1,128)}, bf16[6144,256]{1,0:T(8,128)(2,1)}) custom-call(s32[1]{0:T(128)S(6)} %copy.18.live_ref, s32[16,32]{1,0:T(8,128)} %bitcast.11, s32[1,32]{1,0:T(1,128)} %count_ref.1, s32[16,32]{1,0:T(8,128)} %bitcast.12, f32[16,32]{1,0:T(8,128)} %bitcast.13, ...), custom_call_target="tpu_custom_call" | custom-call | tf_op jit(solution)/shard_map/pallas_call | solution.py:324
  62.2 0.0 copy-start.4
  62.2 0.0 copy-start
  62.2 1.9 %copy-done = bf16[6144,256]{1,0:T(8,128)(2,1)S(1)} copy-done((bf16[6144,256]{1,0:T(8,128)(2,1)S(1)}, bf16[6144,256]{1,0:T(8,128)(2,1)}, u32[]{:S(2)}) %copy-start) | copy-done | bytes 3145752
  64.1 0.0 copy-start.1
  64.1 0.9 %copy-done.1 = bf16[512,256]{1,0:T(8,128)(2,1)S(1)} copy-done((bf16[512,256]{1,0:T(8,128)(2,1)S(1)}, bf16[512,256]{1,0:T(8,128)(2,1)}, u32[]{:S(2)}) %copy-start.1) | copy-done | bytes 262168
  65.0 0.0 copy-start.2
  65.0 0.7 copy-done.2
  65.7 0.0 copy-start.3
  65.7 6.9 %shard_map.148 = (bf16[6144,256]{1,0:T(8,128)(2,1)}, bf16[6144,256]{1,0:T(8,128)(2,1)}) custom-call(f32[32,128]{1,0:T(8,128)S(1)} %copy-done.2, bf16[512,256]{1,0:T(8,128)(2,1)S(1)} %copy-done.1, bf16[6144,256]{1,0:T(8,128)(2,1)S(1)} %copy-done), custom_call_target="tpu_custom_call" | custom-call | tf_op jit(solution)/shard_map/pallas_call | solution.py:373
  72.6 0.0 copy-done.3
  72.6 0.7 copy.19
  73.3 0.0 copy-done.4
  73.3 0.6 copy.20
Async XLA Ops:
  62.2 11.1 %copy-start.4 = (f32[1,256]{1,0:T(1,128)S(1)}, f32[1,256]{1,0:T(1,128)}, u32[]{:S(2)}) copy-start(f32[1,256]{1,0:T(1,128)} %get-tuple-element.16) | copy-start | bytes 3076
  62.2 1.9 %copy-start = (bf16[6144,256]{1,0:T(8,128)(2,1)S(1)}, bf16[6144,256]{1,0:T(8,128)(2,1)}, u32[]{:S(2)}) copy-start(bf16[6144,256]{1,0:T(8,128)(2,1)} %get-tuple-element.13.ig_ref) | copy-start | bytes 9437188
  64.1 0.9 %copy-start.1 = (bf16[512,256]{1,0:T(8,128)(2,1)S(1)}, bf16[512,256]{1,0:T(8,128)(2,1)}, u32[]{:S(2)}) copy-start(bf16[512,256]{1,0:T(8,128)(2,1)} %get-tuple-element.12.arrived_ref) | copy-start | bytes 786436
  65.0 0.7 copy-start.2
  65.7 6.9 %copy-start.3 = (f32[256,256]{1,0:T(8,128)S(1)}, f32[256,256]{1,0:T(8,128)}, u32[]{:S(2)}) copy-start(f32[256,256]{1,0:T(8,128)} %get-tuple-element.23) | copy-start | bytes 786436

commit v2 on v1

--- a/solution.py
+++ b/solution.py
@@ -63,7 +63,7 @@
     wanted_out, arrived_out, wg_out, bg_out, ig_hbm,
     feats, adj, cot, emb, grad, local, fg, ig,
     rq_send, rq_recv, e_send, e_recv, g_send, g_recv, m_send,
-    rs_send, rs_recv, acc, mes, wacc, bacc,
+    rs_send, rs_recv, ws, bs, acc, mes, wacc, bacc,
     load_sem, adj_sem, out_sem, send_sem, recv_sem,
 ):
     nodes_dev, width = feats.shape
@@ -73,7 +73,8 @@
     total = peers * slots
     me = lax.axis_index("group") * members + lax.axis_index("inner")
     part = width // reducers
-    chunk = rs_send.shape[0] // reducers
+    chunk = 2 * part
+    lanes = width // 2
 
     def at(p):
         return (p // members, p % members)
@@ -146,17 +147,20 @@
 
     wait_bytes(rq_recv.at[pl.ds(0, peers - 1)], recv_sem.at[0])
     wanted = jnp.concatenate([rq_recv[p] for p in range(peers)], axis=0)
-    wanted_out[...] = wanted
     pick = (iota((total, peers), 0) // slots == iota((total, peers), 1)).astype(F32)
     wide = exact(pick, wanted)
     keep = iota((total, 128), 0) % slots == iota((total, 128), 1)
     wanted_col = jnp.sum(jnp.where(keep, wide, 0.0), axis=1, keepdims=True).astype(jnp.int32)
+    flat = iota((peers, total), 1) // slots == iota((peers, total), 0)
+    wide = exact(wanted, flat.astype(F32), TN)
+    keep = iota((128, total), 1) % slots == iota((128, total), 0)
+    wanted_out[...] = jnp.sum(jnp.where(keep, wide, 0.0), axis=0, keepdims=True).astype(jnp.int32)
     lane = iota((total, cluster), 1)
 
     def gather(table, out):
         acc[...] = jnp.zeros_like(acc)
 
-        @pl.loop(0, clusters)
+        @pl.loop(0, clusters, unroll=4)
         def _(c):
             one = jnp.where(wanted_col - c * cluster == lane, 1.0, 0.0).astype(BF)
             acc[...] += mm(one, tile(table, c)[...])
@@ -192,7 +196,7 @@
     def live_of(c):
         return jnp.where(c < live_ref[0], 1.0, 0.0).astype(F32)
 
-    @pl.loop(0, clusters)
+    @pl.loop(0, clusters, unroll=3)
     def _(c):
         spread = jnp.where(target_row - c * cluster == node, 1.0, 0.0).astype(BF)
         agg = (tile(local, c)[...] + mm(spread, e_recv[...])).astype(BF)
@@ -200,25 +204,32 @@
         g = tile(cot, c)[...].astype(F32) * gelu_slope(pre) * live_of(c)
         low = g.astype(BF)
         bacc[...] += jnp.sum(g.reshape(cluster // 8, 8, width), axis=0)
-        wacc[...] += mm(agg, low, TN)
+        tile(feats, c)[...] = agg
+        tile(cot, c)[...] = low
         back = mm(low, weights, NT).astype(BF)
         tile(fg, c)[...] = back
         take = jnp.where(target_col - c * cluster == lane, 1.0, 0.0).astype(BF)
         mes[...] += mm(take, back)
 
-    sums = bacc[...].astype(BF).astype(F32)
+    m_send[...] = (scale_col * mes[...]).astype(BF)
+    arrived_out[own, :] = m_send[own, :]
+    to_all(4, rows_at(m_send, slots), rows_at(arrived_out, slots))
+
+    @pl.loop(0, clusters)
+    def _(c):
+        wacc[...] += mm(tile(feats, c)[...], tile(cot, c)[...], TN)
+
+    pairs = []
     for r in range(reducers):
         piece = wacc[r * part : (r + 1) * part, :]
-        fill = chunk - part - 8
-        both = [piece, sums] + ([jnp.zeros((fill, width), F32)] if fill else [])
-        rs_send[r * chunk : (r + 1) * chunk, :] = jnp.concatenate(both, axis=0).astype(BF)
+        pairs += [piece[:, :lanes], piece[:, lanes:]]
+    rs_send[...] = jnp.concatenate(pairs, axis=0).astype(BF)
     slice_of = rows_at(rs_send, chunk)
     slot_of = rows_at(rs_recv, chunk)
     slot_of(me)[...] = slice_of(lax.rem(me, reducers))[...]
     to_all(3, lambda p: slice_of(lax.rem(p, reducers)), slot_of)
-    m_send[...] = (scale_col * mes[...]).astype(BF)
-    arrived_out[own, :] = m_send[own, :]
-    to_all(4, rows_at(m_send, slots), rows_at(arrived_out, slots))
+    bs[me] = jnp.sum(bacc[...], axis=0, keepdims=True)
+    to_all(6, lambda p: bs.at[me], lambda p: bs.at[p])
 
     wait_bytes(g_recv.at[pl.ds(0, (peers - 1) * slots)], recv_sem.at[2])
     scaled = (scale_col * g_recv[...].astype(F32)).astype(BF)
@@ -241,11 +252,9 @@
 
     wait_bytes(rs_recv.at[pl.ds(0, (peers - 1) * chunk)], recv_sem.at[3])
     norm = float(nodes_dev * peers) ** (-0.5)
-    got = jnp.sum(rs_recv[...].astype(F32).reshape(peers, chunk, width), axis=0) * norm
-    mine = lax.rem(me, reducers)
-    part_of = rows_at(wg_out, part)
-    part_of(mine)[...] = got[:part, :]
-    bg_out[...] = jnp.sum(got[part : part + 8, :], axis=0, keepdims=True)
+    got = jnp.sum(rs_recv[...].astype(F32).reshape(peers, chunk, lanes), axis=0) * norm
+    part_of = rows_at(ws, chunk)
+    part_of(lax.rem(me, reducers))[...] = got.astype(BF)
 
     def share():
         to_all(5, lambda p: part_of(me), part_of)
@@ -260,21 +269,27 @@
         backward(c)
 
     if reducers == peers:
-        wait_bytes(wg_out.at[pl.ds(0, (peers - 1) * part)], recv_sem.at[5])
-        wait_bytes(wg_out.at[pl.ds(0, (peers - 1) * part)], send_sem.at[5])
+        wait_bytes(ws.at[pl.ds(0, (peers - 1) * chunk)], recv_sem.at[5])
+        wait_bytes(ws.at[pl.ds(0, (peers - 1) * chunk)], send_sem.at[5])
     else:
         @pl.when(me < reducers)
         def _():
-            wait_bytes(wg_out.at[pl.ds(0, (reducers - 1) * part)], recv_sem.at[5])
+            wait_bytes(ws.at[pl.ds(0, (reducers - 1) * chunk)], recv_sem.at[5])
 
             @pl.loop(1, peers)
             def _(i):
-                wait_bytes(wg_out.at[pl.ds(0, part)], send_sem.at[5])
+                wait_bytes(ws.at[pl.ds(0, chunk)], send_sem.at[5])
 
         @pl.when(me >= reducers)
         def _():
-            wait_bytes(wg_out, recv_sem.at[5])
-
+            wait_bytes(ws, recv_sem.at[5])
+
+    halves = ws[...].astype(F32).reshape(reducers, 2, part, lanes)
+    joined = jnp.concatenate([halves[:, 0], halves[:, 1]], axis=-1)
+    wg_out[...] = joined.reshape(width, width)
+    wait_bytes(bs.at[pl.ds(0, peers - 1)], recv_sem.at[6])
+    wait_bytes(bs.at[pl.ds(0, peers - 1)], send_sem.at[6])
+    bg_out[...] = jnp.sum(bs[...], axis=0) * norm
     wait_bytes(arrived_out.at[pl.ds(0, (peers - 1) * slots)], recv_sem.at[4])
     wait_bytes(rq_send.at[pl.ds(0, peers - 1)], send_sem.at[0])
     wait_bytes(e_send.at[pl.ds(0, (peers - 1) * slots)], send_sem.at[1])
@@ -284,21 +299,19 @@
     wait_bytes(ig, out_sem)
 
 
-def owner_kernel(slots, wanted_ref, arrived_ref, ig_ref, out_ref, ig_out, row_scr):
+def owner_kernel(
+    wanted_ref, arrived_ref, wg_ref, bg_ref, ig_ref, out_ref, ig_out, wg_out, bg_out
+):
     step = pl.program_id(0)
-    peers = wanted_ref.shape[0]
-    total = peers * slots
 
     @pl.when(step == 0)
     def _():
-        pick = (iota((peers, total), 1) // slots == iota((peers, total), 0)).astype(F32)
-        wide = exact(wanted_ref[...], pick, TN)
-        keep = iota((128, total), 1) % slots == iota((128, total), 0)
-        row = jnp.sum(jnp.where(keep, wide, 0.0), axis=0, keepdims=True)
-        row_scr[...] = row.astype(jnp.int32)
+        wg_out[...] = wg_ref[...]
+        bg_out[...] = bg_ref[0]
 
     size = out_ref.shape[0]
-    spread = jnp.where(row_scr[...] - step * size == iota((size, total), 0), 1.0, 0.0)
+    total = arrived_ref.shape[0]
+    spread = jnp.where(wanted_ref[...] - step * size == iota((size, total), 0), 1.0, 0.0)
     out_ref[...] = mm(spread.astype(BF), arrived_ref[...]).astype(BF)
     ig_out[...] = ig_ref[...]
 
@@ -315,7 +328,7 @@
     total = peers * slots
     reducers = min(peers, 32)
     part = width // reducers
-    chunk = -(-(part + 8) // 16) * 16
+    chunk, lanes = 2 * part, width // 2
     flip = lambda a: jnp.transpose(a[0])
     vmem = pl.BlockSpec(memory_space=pltpu.VMEM)
     hbm = pl.BlockSpec(memory_space=pl.ANY)
@@ -324,7 +337,7 @@
     wanted, arrived, wg, bg, ig = pl.pallas_call(
         functools.partial(main_kernel, members, peers, reducers),
         out_shape=(
-            sds((peers, 128), F32),
+            sds((1, total), jnp.int32),
             sds((total, width), BF),
             sds((width, width), F32),
             sds((1, width), F32),
@@ -348,8 +361,10 @@
             pltpu.VMEM((total, width), BF),
             pltpu.VMEM((total, width), BF),
             pltpu.VMEM((total, width), BF),
-            pltpu.VMEM((reducers * chunk, width), BF),
-            pltpu.VMEM((peers * chunk, width), BF),
+            pltpu.VMEM((reducers * chunk, lanes), BF),
+            pltpu.VMEM((peers * chunk, lanes), BF),
+            pltpu.VMEM((reducers * chunk, lanes), BF),
+            pltpu.VMEM((peers, 1, width), F32),
             pltpu.VMEM((total, width), F32),
             pltpu.VMEM((total, width), F32),
             pltpu.VMEM((width, width), F32),
@@ -357,8 +372,8 @@
             pltpu.SemaphoreType.DMA((4,)),
             pltpu.SemaphoreType.DMA((clusters,)),
             pltpu.SemaphoreType.DMA,
-            pltpu.SemaphoreType.DMA((6,)),
-            pltpu.SemaphoreType.DMA((6,)),
+            pltpu.SemaphoreType.DMA((7,)),
+            pltpu.SemaphoreType.DMA((7,)),
         ],
         compiler_params=pltpu.CompilerParams(
             collective_id=0, has_side_effects=True, vmem_limit_bytes=58 * 1024 * 1024
@@ -368,18 +383,19 @@
         layer_weight, layer_bias[None, :],
         node_feats, adj_tiles, cotangent, hist_emb, hist_grad,
     )
-    whole = lambda a: pl.BlockSpec(a.shape, lambda i: (0, 0))
-    tiles = pl.BlockSpec((cluster, width), lambda i: (i, 0))
-    owner_grad, input_grad = pl.pallas_call(
-        functools.partial(owner_kernel, slots),
-        grid=(clusters,),
-        out_shape=(sds(full, BF), sds(full, BF)),
-        in_specs=[whole(wanted), whole(arrived), tiles],
-        out_specs=(tiles, tiles),
-        scratch_shapes=[pltpu.VMEM((1, total), jnp.int32)],
-        compiler_params=pltpu.CompilerParams(vmem_limit_bytes=32 * 1024 * 1024),
-    )(wanted, arrived, ig)
-    return input_grad, wg, bg[0], owner_grad
+    whole = lambda a: pl.BlockSpec(a.shape, lambda i: (0,) * len(a.shape))
+    per_step = 2 if clusters % 2 == 0 else 1
+    tiles = pl.BlockSpec((per_step * cluster, width), lambda i: (i, 0))
+    bias_out = sds((width,), F32)
+    owner_grad, input_grad, weight_grad, bias_grad = pl.pallas_call(
+        owner_kernel,
+        grid=(clusters // per_step,),
+        out_shape=(sds(full, BF), sds(full, BF), sds(wg.shape, F32), bias_out),
+        in_specs=[whole(wanted), whole(arrived), whole(wg), whole(bg), tiles],
+        out_specs=(tiles, tiles, whole(wg), whole(bias_out)),
+        compiler_params=pltpu.CompilerParams(vmem_limit_bytes=60 * 1024 * 1024),
+    )(wanted, arrived, wg, bg, ig)
+    return input_grad, weight_grad, bias_grad, owner_grad
 
 
 def solution(mesh):

time: 74.1 us -> 63.1 us (0.85)
  Pallas kernels: 67.7 us -> 61.6 us
  local copies, waits for them, and re-layouts: 4.82 us -> 0 us
    pallas_call x1, Pallas kernels: 60.9 us -> 54.6 us  [on_device(): pl.pallas_call(functools.partial(main_kernel, members, peers, reducers),...]
    unnamed x12 -> x0, local copies, waits for them, and re-layouts: 4.82 us -> none
where the time goes in v2:
time: 63.1 us; the launch traced here: 62.9 us
  Pallas kernels  61.6 us (98%)
  between operations  1.29 us (2%)
    pallas_call x1, Pallas kernels, on_device(): pl.pallas_call(functools.partial(main_kernel, members, peers, reducers),...  54.6 us
    pallas_call x1, Pallas kernels, on_device(): pl.pallas_call(owner_kernel, grid=(clusters // per_step,), out_shape=(sds...  6.92 us

profile of v2, /device:TPU:0, one launch (start us, length us, event | category | flops | bytes accessed | tf_op | source)
XLA Modules:
  0.0 62.9 jit_solution(159243290529026770)
XLA Ops:
  1.3 54.6 %shard_map.147 = (s32[1,512]{1,0:T(1,128)}, bf16[512,256]{1,0:T(8,128)(2,1)}, f32[256,256]{1,0:T(8,128)}, f32[1,256]{1,0:T(1,128)}, bf16[6144,256]{1,0:T(8,128)(2,1)}) custom-call(s32[1]{0:T(128)S(6)} %copy.16.live_ref, s32[16,32]{1,0:T(8,128)} %bitcast.10, s32[1,32]{1,0:T(1,128)} %count_ref.1, s32[16,32]{1,0:T(8,128)} %bitcast.11, f32[16,32]{1,0:T(8,128)} %bitcast.12, ...), custom_call_target="tpu_custom_call" | custom-call | tf_op jit(solution)/shard_map/pallas_call | solution.py:337
  55.9 6.9 %shard_map.148 = (bf16[6144,256]{1,0:T(8,128)(2,1)}, bf16[6144,256]{1,0:T(8,128)(2,1)}, f32[256,256]{1,0:T(8,128)}, f32[256]{0:T(256)}) custom-call(s32[1,512]{1,0:T(1,128)} %get-tuple-element.13.wanted_ref, bf16[512,256]{1,0:T(8,128)(2,1)} %get-tuple-element.14.arrived_ref, f32[256,256]{1,0:T(8,128)} %get-tuple-element.15.wg_ref, ...), custom_call_target="tpu_custom_call" | custom-call | tf_op jit(solution)/shard_map/pallas_call | solution.py:390

commit v3 on v2

--- a/solution.py
+++ b/solution.py
@@ -60,11 +60,11 @@
     members, peers, reducers,
     live_ref, rows_ref, count_ref, target_ref, weight_ref, w_ref, bias_ref,
     feats_hbm, adj_hbm, cot_hbm, emb_hbm, grad_hbm,
-    wanted_out, arrived_out, wg_out, bg_out, ig_hbm,
+    wg_out, bg_out, ig_hbm, og_hbm,
     feats, adj, cot, emb, grad, local, fg, ig,
     rq_send, rq_recv, e_send, e_recv, g_send, g_recv, m_send,
-    rs_send, rs_recv, ws, bs, acc, mes, wacc, bacc,
-    load_sem, adj_sem, out_sem, send_sem, recv_sem,
+    rs_send, rs_recv, ws, bs, arrived_out, acc, mes, wacc, bacc,
+    load_sem, adj_sem, out_sem, og_sem, send_sem, recv_sem,
 ):
     nodes_dev, width = feats.shape
     cluster = adj.shape[1]
@@ -154,7 +154,7 @@
     flat = iota((peers, total), 1) // slots == iota((peers, total), 0)
     wide = exact(wanted, flat.astype(F32), TN)
     keep = iota((128, total), 1) % slots == iota((128, total), 0)
-    wanted_out[...] = jnp.sum(jnp.where(keep, wide, 0.0), axis=0, keepdims=True).astype(jnp.int32)
+    wanted_row = jnp.sum(jnp.where(keep, wide, 0.0), axis=0, keepdims=True).astype(jnp.int32)
     lane = iota((total, cluster), 1)
 
     def gather(table, out):
@@ -268,6 +268,14 @@
     def _(c):
         backward(c)
 
+    wait_bytes(arrived_out.at[pl.ds(0, (peers - 1) * slots)], recv_sem.at[4])
+
+    @pl.loop(0, clusters, unroll=2)
+    def _(c):
+        spread = jnp.where(wanted_row - c * cluster == node, 1.0, 0.0).astype(BF)
+        tile(emb, c)[...] = mm(spread, arrived_out[...]).astype(BF)
+        pltpu.make_async_copy(tile(emb, c), tile(og_hbm, c), og_sem).start()
+
     if reducers == peers:
         wait_bytes(ws.at[pl.ds(0, (peers - 1) * chunk)], recv_sem.at[5])
         wait_bytes(ws.at[pl.ds(0, (peers - 1) * chunk)], send_sem.at[5])
@@ -290,30 +298,23 @@
     wait_bytes(bs.at[pl.ds(0, peers - 1)], recv_sem.at[6])
     wait_bytes(bs.at[pl.ds(0, peers - 1)], send_sem.at[6])
     bg_out[...] = jnp.sum(bs[...], axis=0) * norm
-    wait_bytes(arrived_out.at[pl.ds(0, (peers - 1) * slots)], recv_sem.at[4])
     wait_bytes(rq_send.at[pl.ds(0, peers - 1)], send_sem.at[0])
     wait_bytes(e_send.at[pl.ds(0, (peers - 1) * slots)], send_sem.at[1])
     wait_bytes(g_send.at[pl.ds(0, (peers - 1) * slots)], send_sem.at[2])
     wait_bytes(rs_recv.at[pl.ds(0, (peers - 1) * chunk)], send_sem.at[3])
     wait_bytes(m_send.at[pl.ds(0, (peers - 1) * slots)], send_sem.at[4])
     wait_bytes(ig, out_sem)
-
-
-def owner_kernel(
-    wanted_ref, arrived_ref, wg_ref, bg_ref, ig_ref, out_ref, ig_out, wg_out, bg_out
-):
-    step = pl.program_id(0)
-
-    @pl.when(step == 0)
+    wait_bytes(emb, og_sem)
+
+
+def pass_kernel(wg_ref, bg_ref, ig_ref, og_ref, ig_out, og_out, wg_out, bg_out):
+    @pl.when(pl.program_id(0) == 0)
     def _():
         wg_out[...] = wg_ref[...]
         bg_out[...] = bg_ref[0]
 
-    size = out_ref.shape[0]
-    total = arrived_ref.shape[0]
-    spread = jnp.where(wanted_ref[...] - step * size == iota((size, total), 0), 1.0, 0.0)
-    out_ref[...] = mm(spread.astype(BF), arrived_ref[...]).astype(BF)
     ig_out[...] = ig_ref[...]
+    og_out[...] = og_ref[...]
 
 
 def on_device(
@@ -334,17 +335,16 @@
     hbm = pl.BlockSpec(memory_space=pl.ANY)
     sds = jax.ShapeDtypeStruct
     full = (nodes_dev, width)
-    wanted, arrived, wg, bg, ig = pl.pallas_call(
+    wg, bg, ig, og = pl.pallas_call(
         functools.partial(main_kernel, members, peers, reducers),
         out_shape=(
-            sds((1, total), jnp.int32),
-            sds((total, width), BF),
             sds((width, width), F32),
             sds((1, width), F32),
             sds(full, BF),
+            sds(full, BF),
         ),
         in_specs=[pl.BlockSpec(memory_space=pltpu.SMEM)] + [vmem] * 6 + [hbm] * 5,
-        out_specs=(vmem, vmem, vmem, vmem, hbm),
+        out_specs=(vmem, vmem, hbm, hbm),
         scratch_shapes=[
             pltpu.VMEM(full, BF),
             pltpu.VMEM((nodes_dev, cluster), BF),
@@ -365,12 +365,14 @@
             pltpu.VMEM((peers * chunk, lanes), BF),
             pltpu.VMEM((reducers * chunk, lanes), BF),
             pltpu.VMEM((peers, 1, width), F32),
+            pltpu.VMEM((total, width), BF),
             pltpu.VMEM((total, width), F32),
             pltpu.VMEM((total, width), F32),
             pltpu.VMEM((width, width), F32),
             pltpu.VMEM((8, width), F32),
             pltpu.SemaphoreType.DMA((4,)),
             pltpu.SemaphoreType.DMA((clusters,)),
+            pltpu.SemaphoreType.DMA,
             pltpu.SemaphoreType.DMA,
             pltpu.SemaphoreType.DMA((7,)),
             pltpu.SemaphoreType.DMA((7,)),
@@ -384,17 +386,17 @@
         node_feats, adj_tiles, cotangent, hist_emb, hist_grad,
     )
     whole = lambda a: pl.BlockSpec(a.shape, lambda i: (0,) * len(a.shape))
-    per_step = 2 if clusters % 2 == 0 else 1
+    per_step = 3 if clusters % 3 == 0 else 1
     tiles = pl.BlockSpec((per_step * cluster, width), lambda i: (i, 0))
     bias_out = sds((width,), F32)
-    owner_grad, input_grad, weight_grad, bias_grad = pl.pallas_call(
-        owner_kernel,
+    input_grad, owner_grad, weight_grad, bias_grad = pl.pallas_call(
+        pass_kernel,
         grid=(clusters // per_step,),
         out_shape=(sds(full, BF), sds(full, BF), sds(wg.shape, F32), bias_out),
-        in_specs=[whole(wanted), whole(arrived), whole(wg), whole(bg), tiles],
+        in_specs=[whole(wg), whole(bg), tiles, tiles],
         out_specs=(tiles, tiles, whole(wg), whole(bias_out)),
         compiler_params=pltpu.CompilerParams(vmem_limit_bytes=60 * 1024 * 1024),
-    )(wanted, arrived, wg, bg, ig)
+    )(wg, bg, ig, og)
     return input_grad, weight_grad, bias_grad, owner_grad
 
 

time: 63.1 us -> 62.1 us (0.984)
  Pallas kernels: 61.6 us -> 60.6 us
    pallas_call x1, Pallas kernels: 6.92 us -> 6.03 us  [on_device(): pl.pallas_call(pass_kernel, grid=(clusters // per_step,), out_shape=(sds(...]
where the time goes in v3:
time: 62.1 us; the launch traced here: 61.9 us
  Pallas kernels  60.6 us (98%)
  between operations  1.29 us (2%)
    pallas_call x1, Pallas kernels, on_device(): pl.pallas_call(functools.partial(main_kernel, members, peers, reducers),...  54.6 us
    pallas_call x1, Pallas kernels, on_device(): pl.pallas_call(pass_kernel, grid=(clusters // per_step,), out_shape=(sds(...  6.03 us

profile of v3, /device:TPU:0, one launch (start us, length us, event | category | flops | bytes accessed | tf_op | source)
XLA Modules:
  0.0 61.9 jit_solution(16795449798227001928)
XLA Ops:
  1.3 54.6 %shard_map.147 = (f32[256,256]{1,0:T(8,128)}, f32[1,256]{1,0:T(1,128)}, bf16[6144,256]{1,0:T(8,128)(2,1)}, bf16[6144,256]{1,0:T(8,128)(2,1)}) custom-call(s32[1]{0:T(128)S(6)} %copy.16.live_ref, s32[16,32]{1,0:T(8,128)} %bitcast.10, s32[1,32]{1,0:T(1,128)} %count_ref.1, s32[16,32]{1,0:T(8,128)} %bitcast.11, f32[16,32]{1,0:T(8,128)} %bitcast.12, ...), custom_call_target="tpu_custom_call" | custom-call | tf_op jit(solution)/shard_map/pallas_call | solution.py:338
  55.9 6.0 %shard_map.148 = (bf16[6144,256]{1,0:T(8,128)(2,1)}, bf16[6144,256]{1,0:T(8,128)(2,1)}, f32[256,256]{1,0:T(8,128)}, f32[256]{0:T(256)}) custom-call(f32[256,256]{1,0:T(8,128)} %get-tuple-element.12.wg_ref, f32[1,256]{1,0:T(1,128)} %get-tuple-element.13.bg_ref, bf16[6144,256]{1,0:T(8,128)(2,1)} %get-tuple-element.14.ig_ref, ...), custom_call_target="tpu_custom_call" | custom-call | tf_op jit(solution)/shard_map/pallas_call | solution.py:392
